TPU v7x, 256 devices: a whole 4x4x8 slice. The times are simulated.
256 devices in a mesh: seq: 64 (over x, y, z_lo, core), state: 4 (over z_hi).
Axes of the slice: x: 4, y: 4, z: 8 (z_hi: 4, z_lo: 2; z = z_hi * 2 + z_lo), core: 2. Of those that a mesh axis runs over, the one named last changes fastest.
Arguments:
- outer_factor: bfloat16 [256, 256, 256], P('state'), may hold values from -0.375 to 0.375
- inner_factor: bfloat16 [256, 256, 256], P('state', 'seq'), may hold values from -0.375 to 0.375
- alpha_start: bfloat16 [256, 65536], P('seq', 'state'), may hold values from -16 to 16
- beta_end: bfloat16 [256, 65536], P('seq', 'state'), may hold values from -6 to 6
- emissions: bfloat16 [4, 256, 65536], P(None, 'seq', 'state'), may hold values from 0.5 to 2
- normalizers: float32 [4, 256], P(None, 'seq'), may hold values from 0.7 to 2
Outputs:
- beta_start: float32 [256, 65536], P('seq', 'state')
- inner_grad: float32 [256, 256, 256], P('state', 'seq')
All inputs are finite; a program needn't handle non-finite values.
Results may differ from a plain program's by a relative error of at most 0.015.
Values may be sent and summed in bfloat16 or wider, within the bound.
A program may use at most 192 MiB of HBM per device.

v0:
```python
import math

import jax
import jax.numpy as jnp
from jax import lax
from jax.sharding import PartitionSpec as P


def local(outer_factor, inner_factor, alpha_start, beta_end, emissions, normalizers):
    local_blocks = outer_factor.shape[0]
    block_size = outer_factor.shape[1]
    row_count = alpha_start.shape[0]
    step_count = emissions.shape[0]

    def as_blocks(flat):
        return flat.reshape(row_count, local_blocks, block_size)

    inner_full = lax.all_gather(inner_factor, "seq", axis=1, tiled=True)

    def reweight(message, step_index):
        scaled = message.astype(jnp.float32) * as_blocks(emissions[step_index]).astype(jnp.float32)
        return (scaled / normalizers[step_index][:, None, None]).astype(jnp.bfloat16)

    inner_inputs = [None] * step_count
    inner_outputs = [None] * step_count
    forward_msg = as_blocks(alpha_start)
    backward_msg = as_blocks(beta_end)
    for step_index in range(step_count):
        spread = lax.all_to_all(
            jnp.einsum(
                "nki,kij->nkj", forward_msg, outer_factor, preferred_element_type=jnp.float32
            ).astype(jnp.bfloat16),
            "state",
            split_axis=2,
            concat_axis=1,
            tiled=True,
        )
        inner_inputs[step_index] = spread
        if step_index + 1 < step_count:
            returned = lax.all_to_all(
                jnp.einsum(
                    "naj,jab->nbj", spread, inner_full, preferred_element_type=jnp.float32
                ).astype(jnp.bfloat16),
                "state",
                split_axis=1,
                concat_axis=2,
                tiled=True,
            )
            forward_msg = reweight(returned, step_index)
    for step_index in reversed(range(step_count)):
        weighted = reweight(backward_msg, step_index)
        spread = lax.all_to_all(weighted, "state", split_axis=2, concat_axis=1, tiled=True)
        inner_outputs[step_index] = spread
        returned = lax.all_to_all(
            jnp.einsum(
                "nbj,jab->naj", spread, inner_full, preferred_element_type=jnp.float32
            ).astype(jnp.bfloat16),
            "state",
            split_axis=1,
            concat_axis=2,
            tiled=True,
        )
        backward_msg = jnp.einsum(
            "nkj,kij->nki", returned, outer_factor, preferred_element_type=jnp.float32
        )
    grad_scale = 1.0 / math.sqrt(row_count * lax.axis_size("seq") * step_count)
    gradient = jnp.zeros((block_size, local_blocks, block_size), jnp.float32)
    for step_index in range(step_count):
        gradient = gradient + jnp.einsum(
            "naj,nbj->ajb",
            inner_inputs[step_index],
            inner_outputs[step_index],
            preferred_element_type=jnp.float32,
        )
    shares = lax.psum_scatter(gradient * grad_scale, "seq", scatter_dimension=0, tiled=True)
    return (backward_msg.reshape(row_count, -1), jnp.transpose(shares, (1, 0, 2)))


def solution(mesh):
    placed = (
        P("state", None, None),
        P("state", "seq", None),
        P("seq", "state"),
        P("seq", "state"),
        P(None, "seq", "state"),
        P(None, "seq"),
    )
    return jax.shard_map(
        local,
        mesh=mesh,
        in_specs=placed,
        out_specs=(P("seq", "state"), P("state", "seq", None)),
        check_vma=False,
    )
```

profile of v0, /device:TPU:1, one launch (start us, length us, event | category | flops | bytes accessed | tf_op | source)
XLA Modules:
  0.0 707.9 jit_solution(6762858205367226238)
XLA Ops:
  7.3 1.7 copy.127
  9.0 4.6 fusion.44
  14.7 9.0 %all-to-all-start.8 = ((bf16[4,2,8192]{2,1,0:T(2,128)(2,1)}), bf16[4,2,8192]{2,1,0:T(2,128)(2,1)S(1)}, u32[]{:S(2)}, u32[]{:S(2)}) async-start(bf16[4,2,8192]{2,1,0:T(2,128)(2,1)} %reshape.66), calls=%async_computation.8 | async-start | bytes 262144 | tf_op jit(solution)/shard_map/all_to_all | solution.py:29
  24.2 0.9 reshape.50
  25.1 5.8 all-to-all-done.8
  30.9 3.3 all-to-all-start
  35.0 7.4 %all-to-all-done = bf16[4,2,8192]{2,1,0:T(2,128)(2,1)S(1)} async-done(((bf16[4,2,8192]{2,1,0:T(2,128)(2,1)}), bf16[4,2,8192]{2,1,0:T(2,128)(2,1)S(1)}, u32[]{:S(2)}, u32[]{:S(2)}) %all-to-all-start) | async-done | bytes 131104 | tf_op jit(solution)/shard_map/all_to_all | solution.py:52
  43.2 85.0 %all-gather.2.cloned.1.call-done = bf16[64,256,256]{2,0,1:T(8,128)(2,1)} async-done(((bf16[64,4,256]{2,0,1:T(8,128)(2,1)}), bf16[64,256,256]{2,0,1:T(8,128)(2,1)}) %all-gather.2.cloned.1.call-update) | async-done | bytes 8388624 | tf_op jit(solution)/shard_map/all_gather | solution.py:18
  128.2 7.9 %fusion.54 = bf16[4,256,64]{1,0,2:T(4,128)(2,1)S(1)} fusion(bf16[4,256,64]{1,0,2:T(4,128)(2,1)S(1)} %all_to_all.212, bf16[64,256,256]{2,0,1:T(8,128)(2,1)} %all-gather.2.cloned.1.call-done), kind=kOutput, calls=%fused_computation.44 | convolution fusion | flops 33619968 | bytes 8650752 | tf_op jit(solution)/shard_map/naj,jab->nbj/dot_general | solution.py:41
  136.3 0.9 reshape.68
  137.2 6.8 all-to-all-start.9
  144.0 7.9 %fusion.66 = bf16[4,256,64]{1,0,2:T(4,128)(2,1)S(1)} fusion(bf16[4,256,64]{1,0,2:T(4,128)(2,1)S(1)} %all_to_all.180, bf16[64,256,256]{2,0,1:T(8,128)(2,1)} %all-gather.2.cloned.1.call-done), kind=kOutput, calls=%fused_computation.48 | convolution fusion | flops 33619968 | bytes 8650752 | tf_op jit(solution)/shard_map/nbj,jab->naj/dot_general | solution.py:55
  152.1 0.9 reshape.52
  153.0 6.6 all-to-all-start.1
  160.5 4.6 fusion.45
  165.4 0.9 reshape.70
  166.9 6.1 all-to-all-start.10
  173.7 5.6 fusion.20
  179.6 0.9 reshape.54
  180.5 6.8 all-to-all-start.2
  188.1 6.4 all-to-all-done.2
  195.3 7.9 %fusion.63 = bf16[4,256,64]{1,0,2:T(4,128)(2,1)S(1)} fusion(bf16[4,256,64]{1,0,2:T(4,128)(2,1)S(1)} %all_to_all.188, bf16[64,256,256]{2,0,1:T(8,128)(2,1)} %all-gather.2.cloned.1.call-done), kind=kOutput, calls=%fused_computation.47 | convolution fusion | flops 33619968 | bytes 8650752 | tf_op jit(solution)/shard_map/nbj,jab->naj/dot_general | solution.py:55
  203.4 0.9 reshape.56
  204.3 3.3 all-to-all-start.3
  207.7 7.9 %fusion.51 = bf16[4,256,64]{1,0,2:T(4,128)(2,1)S(1)} fusion(bf16[4,256,64]{1,0,2:T(4,128)(2,1)S(1)} %all_to_all.217, bf16[64,256,256]{2,0,1:T(8,128)(2,1)} %all-gather.2.cloned.1.call-done), kind=kOutput, calls=%fused_computation.43 | convolution fusion | flops 33619968 | bytes 8650752 | tf_op jit(solution)/shard_map/naj,jab->nbj/dot_general | solution.py:41
  216.7 6.8 all-to-all-start.11
  224.3 5.6 fusion.21
  231.1 6.6 all-to-all-start.4
  238.6 4.6 fusion.46
  245.0 6.0 all-to-all-start.12
  251.8 7.9 %fusion.60 = bf16[4,256,64]{1,0,2:T(4,128)(2,1)S(1)} fusion(bf16[4,256,64]{1,0,2:T(4,128)(2,1)S(1)} %all_to_all.196, bf16[64,256,256]{2,0,1:T(8,128)(2,1)} %all-gather.2.cloned.1.call-done), kind=kOutput, calls=%fused_computation.46 | convolution fusion | flops 33619968 | bytes 8650752 | tf_op jit(solution)/shard_map/nbj,jab->naj/dot_general | solution.py:55
  260.8 7.0 all-to-all-start.5
  268.6 8.1 %fusion.87 = f32[64,256,256]{2,1,0:T(8,128)} fusion(bf16[4,256,64]{1,0,2:T(4,128)(2,1)S(1)} %all_to_all.188, bf16[4,256,64]{1,0,2:T(4,128)(2,1)S(1)} %all_to_all.222), kind=kOutput, calls=%fused_computation.87 | convolution fusion | flops 33554432 | bytes 17039360 | tf_op jit(solution)/shard_map/naj,nbj->ajb/dot_general | solution.py:69
  276.7 7.9 %fusion.48 = bf16[4,256,64]{1,0,2:T(4,128)(2,1)S(1)} fusion(bf16[4,256,64]{1,0,2:T(4,128)(2,1)S(1)} %all_to_all.222, bf16[64,256,256]{2,0,1:T(8,128)(2,1)} %all-gather.2.cloned.1.call-done), kind=kOutput, calls=%fused_computation.42 | convolution fusion | flops 33619968 | bytes 8650752 | tf_op jit(solution)/shard_map/naj,jab->nbj/dot_general | solution.py:41
  285.7 6.6 all-to-all-start.13
  293.2 5.6 fusion.22
  300.0 6.8 all-to-all-start.6
  307.7 4.6 fusion.47
  314.1 6.0 all-to-all-start.14
  320.1 8.1 %fusion.86 = f32[64,256,256]{2,1,0:T(8,128)} fusion(bf16[4,256,64]{1,0,2:T(4,128)(2,1)S(1)} %all_to_all.196, bf16[4,256,64]{1,0,2:T(4,128)(2,1)S(1)} %all_to_all.217), kind=kOutput, calls=%fused_computation.86 | convolution fusion | flops 33554432 | bytes 17039360 | tf_op jit(solution)/shard_map/naj,nbj->ajb/dot_general | solution.py:69
  329.8 8.1 %fusion.85 = f32[64,256,256]{2,1,0:T(8,128)} fusion(bf16[4,256,64]{1,0,2:T(4,128)(2,1)S(1)} %all_to_all.204, bf16[4,256,64]{1,0,2:T(4,128)(2,1)S(1)} %all_to_all.212), kind=kOutput, calls=%fused_computation.85 | convolution fusion | flops 33554432 | bytes 17039360 | tf_op jit(solution)/shard_map/naj,nbj->ajb/dot_general | solution.py:69
  337.9 23.3 %multiply_bitcast_fusion = f32[256,64,256]{0,2,1:T(8,128)} fusion(f32[64,256,256]{2,1,0:T(8,128)} %fusion.87, f32[64,256,256]{2,1,0:T(8,128)} %fusion.85, f32[64,256,256]{2,1,0:T(8,128)} %fusion.86, bf16[4,256,64]{1,0,2:T(4,128)(2,1)S(1)} %all_to_all.180, bf16[4,256,64]{1,0,2:T(4,128)(2,1)S(1)} %all_to_all.227), kind=kOutput, calls=%fused_computation | convolution fusion | flops 50331648 | bytes 67371008 | tf_op jit(solution)/shard_map/naj,nbj->ajb/dot_general | solution.py:69
  361.2 17.7 %copy.164 = f32[256,64,256]{2,1,0:T(8,128)} copy(f32[256,64,256]{0,2,1:T(8,128)} %multiply_bitcast_fusion) | data formatting | bytes 33554432 | tf_op jit(solution)/shard_map/mul | solution.py:75
  379.0 7.9 %fusion.57 = bf16[4,256,64]{1,0,2:T(4,128)(2,1)S(1)} fusion(bf16[4,256,64]{1,0,2:T(4,128)(2,1)S(1)} %all_to_all.204, bf16[64,256,256]{2,0,1:T(8,128)(2,1)} %all-gather.2.cloned.1.call-done), kind=kOutput, calls=%fused_computation.45 | convolution fusion | flops 33619968 | bytes 8650752 | tf_op jit(solution)/shard_map/nbj,jab->naj/dot_general | solution.py:55
  387.3 13.8 %all_to_all.243 = bf16[4,2,8192]{2,1,0:T(2,128)(2,1)S(1)} all-to-all(bf16[4,2,8192]{2,1,0:T(2,128)(2,1)S(1)} %reshape.64), channel_id=1, replica_groups=mesh['seq'=64,'state'=4] {'state'}, dimensions={0} | all-to-all | bytes 262144 | tf_op jit(solution)/shard_map/all_to_all | solution.py:54
  401.9 6.4 fusion.84
  408.3 290.7 %reduce-scatter.2.cloned.1.call-done = f32[4,64,256]{2,1,0:T(8,128)} async-done(((f32[256,64,256]{2,1,0:T(8,128)}), f32[4,64,256]{2,1,0:T(8,128)}) %reduce-scatter.2.cloned.1.call-update) | async-done | bytes 262160 | tf_op jit(solution)/shard_map/reduce_scatter | solution.py:75
  699.0 1.8 copy.165
  (98 shorter events, 24.8 us)
Async XLA Ops:
  7.2 1.8 copy-start
  7.2 16.5 %copy-start.3 = (bf16[4,16384]{1,0:T(4,128)(2,1)S(1)}, bf16[4,16384]{1,0:T(4,128)(2,1)}, u32[]{:S(2)}) copy-start(bf16[4,16384]{1,0:T(4,128)(2,1)} %param.9) | copy-start | bytes 393220
  7.2 16.5 %copy-start.4 = (f32[4,4]{1,0:T(4,128)S(1)}, f32[4,4]{1,0:T(4,128)}, u32[]{:S(2)}) copy-start(f32[4,4]{1,0:T(4,128)} %param.11) | copy-start | bytes 196
  7.2 16.5 %copy-start.2 = (bf16[4,4,16384]{2,1,0:T(4,128)(2,1)S(1)}, bf16[4,4,16384]{2,1,0:T(4,128)(2,1)}, u32[]{:S(2)}) copy-start(bf16[4,4,16384]{2,1,0:T(4,128)(2,1)} %param.10) | copy-start | bytes 1572868
  7.2 121.0 %all-gather.2.cloned.1.call-start = ((), (), s32[]{:S(2)}) async-start(), calls=%async_computation.16 | async-start | bytes 8519680 | tf_op jit(solution)/shard_map/all_gather | solution.py:18
  14.7 16.2 %all-to-all-start.8 = ((bf16[4,2,8192]{2,1,0:T(2,128)(2,1)}), bf16[4,2,8192]{2,1,0:T(2,128)(2,1)S(1)}, u32[]{:S(2)}, u32[]{:S(2)}) async-start(bf16[4,2,8192]{2,1,0:T(2,128)(2,1)} %reshape.66), calls=%async_computation.8 | async-start | bytes 262144 | tf_op jit(solution)/shard_map/all_to_all | solution.py:29
  30.9 11.5 %all-to-all-start = ((bf16[4,2,8192]{2,1,0:T(2,128)(2,1)}), bf16[4,2,8192]{2,1,0:T(2,128)(2,1)S(1)}, u32[]{:S(2)}, u32[]{:S(2)}) async-start(bf16[4,2,8192]{2,1,0:T(2,128)(2,1)} %reshape.50), calls=%async_computation | async-start | bytes 262144 | tf_op jit(solution)/shard_map/all_to_all | solution.py:52
  137.2 15.8 %all-to-all-start.9 = ((bf16[4,2,8192]{2,1,0:T(2,128)(2,1)}), bf16[4,2,8192]{2,1,0:T(2,128)(2,1)S(1)}, u32[]{:S(2)}, u32[]{:S(2)}) async-start(bf16[4,2,8192]{2,1,0:T(2,128)(2,1)} %reshape.68), calls=%async_computation.9 | async-start | bytes 262144 | tf_op jit(solution)/shard_map/all_to_all | solution.py:40
  153.0 13.9 %all-to-all-start.1 = ((bf16[4,2,8192]{2,1,0:T(2,128)(2,1)}), bf16[4,2,8192]{2,1,0:T(2,128)(2,1)S(1)}, u32[]{:S(2)}, u32[]{:S(2)}) async-start(bf16[4,2,8192]{2,1,0:T(2,128)(2,1)} %reshape.52), calls=%async_computation.1 | async-start | bytes 262144 | tf_op jit(solution)/shard_map/all_to_all | solution.py:54
  166.9 13.6 %all-to-all-start.10 = ((bf16[4,2,8192]{2,1,0:T(2,128)(2,1)}), bf16[4,2,8192]{2,1,0:T(2,128)(2,1)S(1)}, u32[]{:S(2)}, u32[]{:S(2)}) async-start(bf16[4,2,8192]{2,1,0:T(2,128)(2,1)} %reshape.70), calls=%async_computation.10 | async-start | bytes 262144 | tf_op jit(solution)/shard_map/all_to_all | solution.py:29
  180.5 14.0 %all-to-all-start.2 = ((bf16[4,2,8192]{2,1,0:T(2,128)(2,1)}), bf16[4,2,8192]{2,1,0:T(2,128)(2,1)S(1)}, u32[]{:S(2)}, u32[]{:S(2)}) async-start(bf16[4,2,8192]{2,1,0:T(2,128)(2,1)} %reshape.54), calls=%async_computation.2 | async-start | bytes 262144 | tf_op jit(solution)/shard_map/all_to_all | solution.py:52
  204.3 12.3 %all-to-all-start.3 = ((bf16[4,2,8192]{2,1,0:T(2,128)(2,1)}), bf16[4,2,8192]{2,1,0:T(2,128)(2,1)S(1)}, u32[]{:S(2)}, u32[]{:S(2)}) async-start(bf16[4,2,8192]{2,1,0:T(2,128)(2,1)} %reshape.56), calls=%async_computation.3 | async-start | bytes 262144 | tf_op jit(solution)/shard_map/all_to_all | solution.py:54
  216.7 14.4 %all-to-all-start.11 = ((bf16[4,2,8192]{2,1,0:T(2,128)(2,1)}), bf16[4,2,8192]{2,1,0:T(2,128)(2,1)S(1)}, u32[]{:S(2)}, u32[]{:S(2)}) async-start(bf16[4,2,8192]{2,1,0:T(2,128)(2,1)} %reshape.72), calls=%async_computation.11 | async-start | bytes 262144 | tf_op jit(solution)/shard_map/all_to_all | solution.py:40
  231.1 14.0 %all-to-all-start.4 = ((bf16[4,2,8192]{2,1,0:T(2,128)(2,1)}), bf16[4,2,8192]{2,1,0:T(2,128)(2,1)S(1)}, u32[]{:S(2)}, u32[]{:S(2)}) async-start(bf16[4,2,8192]{2,1,0:T(2,128)(2,1)} %reshape.58), calls=%async_computation.4 | async-start | bytes 262144 | tf_op jit(solution)/shard_map/all_to_all | solution.py:52
  245.0 15.8 %all-to-all-start.12 = ((bf16[4,2,8192]{2,1,0:T(2,128)(2,1)}), bf16[4,2,8192]{2,1,0:T(2,128)(2,1)S(1)}, u32[]{:S(2)}, u32[]{:S(2)}) async-start(bf16[4,2,8192]{2,1,0:T(2,128)(2,1)} %reshape.74), calls=%async_computation.12 | async-start | bytes 262144 | tf_op jit(solution)/shard_map/all_to_all | solution.py:29
  260.8 25.0 %all-to-all-start.5 = ((bf16[4,2,8192]{2,1,0:T(2,128)(2,1)}), bf16[4,2,8192]{2,1,0:T(2,128)(2,1)S(1)}, u32[]{:S(2)}, u32[]{:S(2)}) async-start(bf16[4,2,8192]{2,1,0:T(2,128)(2,1)} %reshape.60), calls=%async_computation.5 | async-start | bytes 262144 | tf_op jit(solution)/shard_map/all_to_all | solution.py:54
  285.7 14.2 %all-to-all-start.13 = ((bf16[4,2,8192]{2,1,0:T(2,128)(2,1)}), bf16[4,2,8192]{2,1,0:T(2,128)(2,1)S(1)}, u32[]{:S(2)}, u32[]{:S(2)}) async-start(bf16[4,2,8192]{2,1,0:T(2,128)(2,1)} %reshape.76), calls=%async_computation.13 | async-start | bytes 262144 | tf_op jit(solution)/shard_map/all_to_all | solution.py:40
  300.0 14.1 %all-to-all-start.6 = ((bf16[4,2,8192]{2,1,0:T(2,128)(2,1)}), bf16[4,2,8192]{2,1,0:T(2,128)(2,1)S(1)}, u32[]{:S(2)}, u32[]{:S(2)}) async-start(bf16[4,2,8192]{2,1,0:T(2,128)(2,1)} %reshape.62), calls=%async_computation.6 | async-start | bytes 262144 | tf_op jit(solution)/shard_map/all_to_all | solution.py:52
  314.1 14.9 %all-to-all-start.14 = ((bf16[4,2,8192]{2,1,0:T(2,128)(2,1)}), bf16[4,2,8192]{2,1,0:T(2,128)(2,1)S(1)}, u32[]{:S(2)}, u32[]{:S(2)}) async-start(bf16[4,2,8192]{2,1,0:T(2,128)(2,1)} %reshape.78), calls=%async_computation.14 | async-start | bytes 262144 | tf_op jit(solution)/shard_map/all_to_all | solution.py:29
  320.1 378.9 %reduce-scatter.2.cloned.1.call-start = ((), (), s32[]{:S(2)}) async-start(), calls=%async_computation.17 | async-start | bytes 17039360 | tf_op jit(solution)/shard_map/reduce_scatter | solution.py:75
  378.9 321.9 %copy-start.1 = (bf16[4,16384]{1,0:T(4,128)(2,1)S(1)}, bf16[4,16384]{1,0:T(4,128)(2,1)}, u32[]{:S(2)}) copy-start(bf16[4,16384]{1,0:T(4,128)(2,1)} %param.8) | copy-start | bytes 393220
Sparse Core Ops, SparseCore 0:
  10.5 117.6 all-gather.1
  379.1 319.9 reduce-scatter.1
where the time goes:
time: 721 us; the launch traced here: 708 us
  waiting for transfers between devices  397 us (55%)
  matrix products  145 us (20%)
  starting transfers between devices  87.9 us (12%)
  local copies, waits for them, and re-layouts  49.2 us (7%)
  between operations  14.8 us (2%)
  blocking collectives  13.8 us (2%)
    reduce_scatter x1, waiting for transfers between devices, local(): lax.psum_scatter(gradient * grad_scale, 'seq', scatter_dimension=0, tiled...  291 us
    all_gather x1, waiting for transfers between devices, local(): inner_full = lax.all_gather(inner_factor, 'seq', axis=1, tiled=True)  85 us
    dot_general x4, matrix products, local(): jnp.einsum('naj,nbj->ajb', inner_inputs[step_index], inner_outputs[step_i...  47.7 us
    dot_general x4, matrix products, local(): jnp.einsum('nbj,jab->naj', spread, inner_full, preferred_element_type=jnp...  31.6 us
    all_to_all x4, starting transfers between devices, local(): lax.all_to_all(jnp.einsum('nki,kij->nkj', forward_msg, outer_factor, pref...  27.1 us
    dot_general x3, matrix products, local(): jnp.einsum('naj,jab->nbj', spread, inner_full, preferred_element_type=jnp...  23.7 us
    all_to_all x4, starting transfers between devices, local(): lax.all_to_all(weighted, 'state', split_axis=2, concat_axis=1, tiled=True)  23.6 us
    dot_general x4, matrix products, local(): jnp.einsum('nkj,kij->nki', returned, outer_factor, preferred_element_type...  23.3 us
  transfers between devices with their start and end apart: 16, of which 8 were waited for; matrix products, arithmetic and copies ran while one was open for 17% of the time, Pallas kernels for 0%

commit v1 on v0

v1 whole, which is shorter than its diff:
```python
import functools

import jax
import jax.numpy as jnp
from jax import lax
from jax.experimental import pallas as pl
from jax.experimental.pallas import tpu as pltpu
from jax.sharding import PartitionSpec as P

MESH = pl.DeviceIdType.MESH
F32, BF16 = jnp.float32, jnp.bfloat16

GROUP = 8
PEERS = 32
SEQ = 64
STEPS = 4


def iota(shape, dim):
    return lax.broadcasted_iota(jnp.int32, shape, dim)


def kernel(
    norm_ref, outer_hbm, inner_ref, alpha_ref, beta_ref, emis_ref,
    beta_out, grad_out,
    outer_nat, outer_tr, inner_nat, inner_tr, gathered, sent, received, grad_sent, grad_received,
    ins_tr, outs, rows_in, rows_out,
    load_sem, send_sem, recv_sem, gather_send, gather_recv, grad_send, grad_recv,
):
    seq, state = lax.axis_index("seq"), lax.axis_index("state")
    x = lax.div(seq, 16)
    y = lax.rem(lax.div(seq, 4), 4)
    low = lax.rem(lax.div(seq, 2), 2)
    core = lax.rem(seq, 2)
    place = y * 2 + core
    me = state * GROUP + place

    load = pltpu.make_async_copy(outer_hbm, outer_nat, load_sem)
    load.start()

    xs = [lax.rem(x + d, 4) for d in range(4)]
    ys = [lax.rem(y + d, 4) for d in range(4)]
    lows = [low, 1 - low]
    cores = [core, 1 - core]
    states = [lax.rem(state + d, 4) for d in range(4)]
    far = (2, 1, 3, 0)
    peers = [
        (states[ds] * GROUP + ys[dy] * 2 + cores[dc], x * 16 + ys[dy] * 4 + low * 2 + cores[dc], states[ds], ds)
        for ds in far for dy in far for dc in (1, 0) if ds or dy or dc
    ]
    mates = [
        (xs[dx] * 16 + ys[dy] * 4 + lows[dl] * 2 + cores[dc], ys[dy] * 2 + cores[dc], dx)
        for dx in far for dy in far for dl in (1, 0) for dc in (1, 0) if dx or dy or dl or dc
    ]

    barrier = pltpu.get_barrier_semaphore()
    greeted = 0
    for _, to_seq, to_state, ds in peers:
        if ds:
            pl.semaphore_signal(barrier, 1, device_id=(to_seq, to_state), device_id_type=MESH)
            greeted += 1
    for to_seq, _, _ in mates:
        pl.semaphore_signal(barrier, 1, device_id=(to_seq, state), device_id_type=MESH)
        greeted += 1

    def send(slot):
        for to, to_seq, to_state, _ in peers:
            pltpu.make_async_remote_copy(
                src_ref=sent.at[slot, to],
                dst_ref=received.at[slot, me],
                send_sem=send_sem.at[slot],
                recv_sem=recv_sem.at[slot],
                device_id=(to_seq, to_state),
                device_id_type=MESH,
            ).start()
        received[slot, pl.ds(me, 1)] = sent[slot, pl.ds(me, 1)]

    def wait(slot):
        others = received.at[slot, pl.ds(0, PEERS - 1)]
        pltpu.make_async_copy(others, others, recv_sem.at[slot]).wait()

    low_half = iota((128, 128), 1) < 64

    def swap(a):
        return pltpu.roll(a, 64, 1)

    def at_inner(slot):
        a = [received[slot, s * GROUP : (s + 1) * GROUP].astype(F32).reshape(128, 128) for s in range(4)]
        top = [jnp.where(low_half, a[0], swap(a[1])), jnp.where(low_half, a[2], swap(a[3]))]
        bottom = [jnp.where(low_half, swap(a[0]), a[1]), jnp.where(low_half, swap(a[2]), a[3])]
        return jnp.concatenate([jnp.concatenate(top, axis=1), jnp.concatenate(bottom, axis=1)], axis=0)

    def from_inner(o, slot):
        for u in range(2):
            even, odd = o[:128, u * 128 : (u + 1) * 128], o[128:, u * 128 : (u + 1) * 128]
            first = jnp.where(low_half, even, swap(odd))
            second = jnp.where(low_half, swap(even), odd)
            sent[slot, 2 * u * GROUP : (2 * u + 1) * GROUP] = first.astype(BF16).reshape(GROUP, 16, 128)
            sent[slot, (2 * u + 1) * GROUP : (2 * u + 2) * GROUP] = second.astype(BF16).reshape(GROUP, 16, 128)

    def through_inner(a, factor):
        block = lax.rem(iota((256, 256), 0), 8)
        spread = jnp.concatenate([jnp.where(block == b, a, 0.0).astype(BF16) for b in range(8)], axis=1)
        return jnp.dot(spread, factor[...], preferred_element_type=F32)

    def at_outer(slot):
        a = received[slot].astype(F32)
        both = jnp.concatenate([a[:, :8].reshape(256, 128), a[:, 8:].reshape(256, 128)], axis=1)
        return both.T

    def from_outer(a, slot):
        t = a.T.reshape(PEERS, 8, 256)
        sent[slot] = jnp.concatenate([t[:, :, :128], t[:, :, 128:]], axis=1).astype(BF16)

    def through_outer(a, factor):
        rows_in[...] = a

        def sixteen(g, carry):
            parts = [rows_in[pl.ds(pl.multiple_of(n * 64 + g * 16, 16), 16), :] for n in range(4)]
            part = jnp.concatenate(parts, axis=0)
            block = lax.rem(iota((64, 256), 0), 16)
            spread = jnp.concatenate([jnp.where(block == b, part, 0.0).astype(BF16) for b in range(16)], axis=1)
            o = jnp.dot(
                spread, factor[pl.ds(pl.multiple_of(g * 4096, 4096), 4096), :], preferred_element_type=F32
            )
            for n in range(4):
                rows_out[pl.ds(pl.multiple_of(n * 64 + g * 16, 16), 16), :] = o[n * 16 : (n + 1) * 16]
            return carry

        lax.fori_loop(0, 4, sixteen, 0)
        return rows_out[...]

    def reweight(a, step):
        scaled = a * emis_ref[step].astype(F32)
        return jnp.concatenate(
            [scaled[n * 64 : (n + 1) * 64] / jnp.full((64, 256), norm_ref[step, n], F32) for n in range(4)], axis=0
        )

    def regroup(transposed):
        r, c = iota((512, 512), 1 if transposed else 0), iota((512, 512), 0 if transposed else 1)
        return jnp.where(c == (r // 4) % 16 * 32 + r // 64 * 4 + r % 4, 1.0, 0.0).astype(BF16)

    from_outer(reweight(beta_ref[...].astype(F32), STEPS - 1), 0)
    pl.semaphore_wait(barrier, greeted)
    send(0)
    for to_seq, to_place, _ in mates:
        pltpu.make_async_remote_copy(
            src_ref=inner_ref.at[to_place],
            dst_ref=gathered.at[seq],
            send_sem=gather_send,
            recv_sem=gather_recv,
            device_id=(to_seq, state),
            device_id_type=MESH,
        ).start()
    gathered[pl.ds(seq, 1)] = inner_ref[pl.ds(place, 1)]

    load.wait()
    from_outer(through_outer(alpha_ref[...].astype(F32), outer_nat), 8)
    send(8)

    def turn(k, carry):
        at = pl.ds(pl.multiple_of(k * 256, 256), 256)
        outer_tr[at, :] = outer_nat[at, :].T
        return carry

    lax.fori_loop(0, 64, turn, 0)

    def wait_mates(ref, sem):
        others = ref.at[pl.ds(0, SEQ - 1)]
        pltpu.make_async_copy(others, others, sem).wait()

    wait_mates(gathered, gather_recv)
    move = regroup(False)
    for c in range(4):
        o = jnp.dot(move, gathered[c * 16 : (c + 1) * 16].reshape(512, 256), preferred_element_type=F32)
        for b in range(8):
            inner_nat[b * 256 + c * 64 : b * 256 + (c + 1) * 64, :] = o[b * 64 : (b + 1) * 64].astype(BF16)
    for b in range(8):
        inner_tr[b * 256 : (b + 1) * 256, :] = inner_nat[b * 256 : (b + 1) * 256, :].T

    def backward_inner(t):
        wait(t)
        a = at_inner(t)
        outs[STEPS - 1 - t] = a.astype(BF16)
        from_inner(through_inner(a, inner_tr), 4 + t)
        send(4 + t)

    def forward_arrives(t):
        wait(8 + t)
        a = at_inner(8 + t)
        ins_tr[t] = a.T.astype(BF16)
        return a

    def step(t, carry):
        backward_inner(t)
        from_inner(through_inner(forward_arrives(t), inner_nat), 12 + t)
        send(12 + t)
        wait(4 + t)
        from_outer(reweight(through_outer(at_outer(4 + t), outer_tr), STEPS - 2 - t), t + 1)
        send(t + 1)
        wait(12 + t)
        from_outer(through_outer(reweight(at_outer(12 + t), t), outer_nat), 9 + t)
        send(9 + t)
        return carry

    lax.fori_loop(0, STEPS - 1, step, 0)

    backward_inner(STEPS - 1)
    forward_arrives(STEPS - 1)

    move_back = regroup(True)
    lane_block = lax.rem(iota((64, 256), 1), 8)
    for dx in far:
        c = xs[dx]
        spread = []
        for t in range(STEPS):
            part = ins_tr[t, pl.ds(pl.multiple_of(c * 64, 64), 64), :].astype(F32)
            spread.append(
                jnp.concatenate([jnp.where(lane_block == b, part, 0.0).astype(BF16) for b in range(8)], axis=0)
            )
        g = jnp.dot(jnp.concatenate(spread, axis=1), outs[...].reshape(STEPS * 256, 256), preferred_element_type=F32)
        g = jnp.dot(move_back, g.astype(BF16), preferred_element_type=F32).astype(BF16)
        grad_sent[pl.ds(pl.multiple_of(c * 16, 16), 16)] = g.reshape(16, 32, 256)
        for to_seq, _, to_dx in mates:
            if to_dx == dx:
                pltpu.make_async_remote_copy(
                    src_ref=grad_sent.at[to_seq],
                    dst_ref=grad_received.at[seq],
                    send_sem=grad_send,
                    recv_sem=grad_recv,
                    device_id=(to_seq, state),
                    device_id_type=MESH,
                ).start()
    grad_received[pl.ds(seq, 1)] = grad_sent[pl.ds(seq, 1)]

    wait(STEPS + 3)
    beta_out[...] = through_outer(at_outer(STEPS + 3), outer_tr)

    wait_mates(grad_received, grad_recv)
    for q in range(GROUP):
        total = None
        for xx in range(4):
            for ll in range(2):
                share = grad_received[xx * 16 + q // 2 * 4 + ll * 2 + q % 2].astype(F32)
                total = share if total is None else total + share
        grad_out[q * 32 : (q + 1) * 32, :] = total * (1.0 / 32.0)

    for slot in range(15):
        others = sent.at[slot, pl.ds(0, PEERS - 1)]
        pltpu.make_async_copy(others, others, send_sem.at[slot]).wait()
    wait_mates(gathered, gather_send)
    wait_mates(grad_sent, grad_send)


def local(outer_factor, inner_factor, alpha_start, beta_end, emissions, normalizers):
    vmem, hbm = pl.BlockSpec(memory_space=pltpu.VMEM), pl.BlockSpec(memory_space=pl.ANY)
    beta_start, grad = pl.pallas_call(
        kernel,
        out_shape=(jax.ShapeDtypeStruct((256, 256), F32), jax.ShapeDtypeStruct((256, 256), F32)),
        in_specs=[pl.BlockSpec(memory_space=pltpu.SMEM), hbm, vmem, vmem, vmem, vmem],
        out_specs=(vmem, vmem),
        scratch_shapes=[
            pltpu.VMEM((64 * 256, 256), BF16),
            pltpu.VMEM((64 * 256, 256), BF16),
            pltpu.VMEM((8 * 256, 256), BF16),
            pltpu.VMEM((8 * 256, 256), BF16),
            pltpu.VMEM((SEQ, 32, 256), BF16),
            pltpu.VMEM((15, PEERS, 16, 128), BF16),
            pltpu.VMEM((15, PEERS, 16, 128), BF16),
            pltpu.VMEM((SEQ, 32, 256), BF16),
            pltpu.VMEM((SEQ, 32, 256), BF16),
            pltpu.VMEM((STEPS, 256, 256), BF16),
            pltpu.VMEM((STEPS, 256, 256), BF16),
            pltpu.VMEM((256, 256), F32),
            pltpu.VMEM((256, 256), F32),
            pltpu.SemaphoreType.DMA,
            pltpu.SemaphoreType.DMA((15,)),
            pltpu.SemaphoreType.DMA((15,)),
            pltpu.SemaphoreType.DMA,
            pltpu.SemaphoreType.DMA,
            pltpu.SemaphoreType.DMA,
            pltpu.SemaphoreType.DMA,
        ],
        compiler_params=pltpu.CompilerParams(
            collective_id=0, has_side_effects=True, vmem_limit_bytes=56 * 1024 * 1024
        ),
    )(
        normalizers,
        outer_factor.reshape(64 * 256, 256),
        inner_factor.reshape(GROUP, 32, 256),
        alpha_start.reshape(256, 256),
        beta_end.reshape(256, 256),
        emissions.reshape(STEPS, 256, 256),
    )
    return beta_start.reshape(alpha_start.shape), grad.reshape(inner_factor.shape)


def solution(mesh):
    placed = (
        P("state", None, None),
        P("state", "seq", None),
        P("seq", "state"),
        P("seq", "state"),
        P(None, "seq", "state"),
        P(None, "seq"),
    )
    return jax.shard_map(
        local,
        mesh=mesh,
        in_specs=placed,
        out_specs=(P("seq", "state"), P("state", "seq", None)),
        check_vma=False,
    )
```

time: 721 us -> 112 us (0.16); the launches traced: 708 us -> 111 us
  waiting for transfers between devices: 397 us -> 0 us
  matrix products: 145 us -> 0 us
  Pallas kernels: 0 us -> 100 us
  starting transfers between devices: 87.9 us -> 0 us
  local copies, waits for them, and re-layouts: 49.2 us -> 10.5 us
  between operations: 14.8 us -> 0.64 us
  blocking collectives: 13.8 us -> 0 us
    reduce_scatter x1 -> x0, waiting for transfers between devices: 291 us -> none  [local(): lax.psum_scatter(gradient * grad_scale, 'seq', scatter_dimension=0, tiled...]
    dot_general x19 -> x0, matrix products: 145 us -> none  [the longest x4 47.7 us: local(): jnp.einsum('naj,nbj->ajb', inner_inputs[step_index], inner_outputs[step_i...]
    pallas_call x0 -> x1, Pallas kernels: none -> 100 us  [local(): pl.pallas_call(kernel, out_shape=(jax.ShapeDtypeStruct((256, 256), F32),...]
    all_to_all x14 -> x0, starting transfers between devices: 87.9 us -> none  [the longest x4 27.1 us: local(): lax.all_to_all(jnp.einsum('nki,kij->nkj', forward_msg, outer_factor, pref...]
    all_gather x1 -> x0, waiting for transfers between devices: 85 us -> none  [local(): inner_full = lax.all_gather(inner_factor, 'seq', axis=1, tiled=True)]
    all_to_all x14 -> x0, waiting for transfers between devices: 21.6 us -> none  [the longest x4 15.1 us: local(): lax.all_to_all(weighted, 'state', split_axis=2, concat_axis=1, tiled=True)]
    unnamed x42 -> x0, local copies, waits for them, and re-layouts: 19.5 us -> none
    mul x1 -> x0, local copies, waits for them, and re-layouts: 17.7 us -> none  [local(): gradient * grad_scale]
  transfers between devices with their start and end apart: 16 -> 0, of which waited for: 8 -> 0; matrix products, arithmetic and copies ran while one was open for 17% -> 0% of each run, Pallas kernels for 0% -> 0%
where the time goes in v1:
time: 112 us; the launch traced here: 111 us
  Pallas kernels  100 us (89%)
  local copies, waits for them, and re-layouts  10.5 us (9%)
    pallas_call x1, Pallas kernels, local(): pl.pallas_call(kernel, out_shape=(jax.ShapeDtypeStruct((256, 256), F32),...  100 us

profile of v1, /device:TPU:1, one launch (start us, length us, event | category | flops | bytes accessed | tf_op | source)
XLA Modules:
  0.0 111.3 jit_solution(18252976292703601708)
XLA Ops:
  0.6 1.6 %reshape.26.inner_ref = bf16[8,32,256]{2,1,0:T(8,128)(2,1)} reshape(bf16[64,4,256]{2,1,0:T(4,128)(2,1)} %param.7) | data formatting | bytes 262144 | tf_op jit(solution)/shard_map/reshape | solution.py:290
  2.2 1.6 %reshape.27.alpha_ref = bf16[256,256]{1,0:T(8,128)(2,1)} reshape(bf16[4,16384]{1,0:T(4,128)(2,1)} %param.8) | data formatting | bytes 262144 | tf_op jit(solution)/shard_map/reshape | solution.py:291
  3.9 1.6 %reshape.28.beta_ref = bf16[256,256]{1,0:T(8,128)(2,1)} reshape(bf16[4,16384]{1,0:T(4,128)(2,1)} %param.9) | data formatting | bytes 262144 | tf_op jit(solution)/shard_map/reshape | solution.py:292
  5.5 2.2 %reshape.29.emis_ref = bf16[4,256,256]{2,1,0:T(8,128)(2,1)} reshape(bf16[4,4,16384]{2,1,0:T(4,128)(2,1)} %param.10) | data formatting | bytes 1048576 | tf_op jit(solution)/shard_map/reshape | solution.py:293
  7.7 100.1 %shard_map.77 = (f32[256,256]{1,0:T(8,128)}, f32[256,256]{1,0:T(8,128)}) custom-call(f32[4,4]{1,0:T(4,128)} %norm_ref.1, bf16[16384,256]{1,0:T(8,128)(2,1)} %bitcast.1, bf16[8,32,256]{2,1,0:T(8,128)(2,1)} %reshape.26.inner_ref, bf16[256,256]{1,0:T(8,128)(2,1)} %reshape.27.alpha_ref, bf16[256,256]{1,0:T(8,128)(2,1)} %reshape.28.beta_ref, ...), custom_call_target="tpu_custom_call" | custom-call | tf_op jit(solution)/shard_map/pallas_call | solution.py:257
  107.8 1.8 %reshape.30 = f32[4,16384]{1,0:T(4,128)} reshape(f32[256,256]{1,0:T(8,128)} %get-tuple-element.4) | data formatting | bytes 524288 | tf_op jit(solution)/shard_map/reshape | solution.py:295
  109.5 1.7 %reshape.31 = f32[64,4,256]{2,1,0:T(4,128)} reshape(f32[256,256]{1,0:T(8,128)} %get-tuple-element.5) | data formatting | bytes 524288 | tf_op jit(solution)/shard_map/reshape | solution.py:295

commit v2 on v1

v2 whole, which is shorter than its diff:
```python
import functools

import jax
import jax.numpy as jnp
from jax import lax
from jax.experimental import pallas as pl
from jax.experimental.pallas import tpu as pltpu
from jax.sharding import PartitionSpec as P

MESH = pl.DeviceIdType.MESH
F32, BF16 = jnp.float32, jnp.bfloat16

GROUP = 8
PEERS = 32
SEQ = 64
STEPS = 4


def iota(shape, dim):
    return lax.broadcasted_iota(jnp.int32, shape, dim)


def kernel(
    norm_ref, outer_hbm, inner_ref, alpha_ref, beta_ref, emis_ref,
    beta_out, grad_out,
    outer_nat, outer_tr, inner_nat, inner_tr, slab, relay, gathered, sent, received, rows_sent, rows_received,
    grad_sent, emis, rows_in, rows_out, mixed,
    load_sem, send_sem, recv_sem, relay_send, relay_recv, gather_send, gather_recv, core_send, core_recv,
    rows_send, rows_recv, grad_send, grad_recv, grad_own,
):
    seq, state = lax.axis_index("seq"), lax.axis_index("state")
    x = lax.div(seq, 16)
    y = lax.rem(lax.div(seq, 4), 4)
    low = lax.rem(lax.div(seq, 2), 2)
    core = lax.rem(seq, 2)
    place = y * 2 + low
    share = x * 2 + core
    me = state * GROUP + place

    load = pltpu.make_async_copy(outer_hbm, outer_nat, load_sem)
    load.start()

    def hops(d, n):
        return min(d, n - d)

    xs = [lax.rem(x + d, 4) for d in range(4)]
    ys = [lax.rem(y + d, 4) for d in range(4)]
    lows = [low, 1 - low]
    cores = [core, 1 - core]
    zs = [lax.rem(state * 2 + low + d, 8) for d in range(8)]
    far = (2, 1, 3, 0)
    peers = []
    for dz in sorted(range(8), key=lambda d: -hops(d, 8)):
        for dy in far:
            if dz or dy:
                to_state, to_low = lax.div(zs[dz], 2), lax.rem(zs[dz], 2)
                to_place = ys[dy] * 2 + to_low
                peers.append((to_state * GROUP + to_place, x * 16 + ys[dy] * 4 + to_low * 2 + core, to_state))
    mates = [
        xs[dx] * 16 + ys[dy] * 4 + lows[dl] * 2 + cores[dc]
        for dx in far for dy in far for dl in (1, 0) for dc in (1, 0) if dx or dy or dl or dc
    ]
    sharers = [
        (xs[dx] * 2 + cores[dc], xs[dx] * 16 + y * 4 + low * 2 + cores[dc])
        for dx in far for dc in (1, 0) if dx or dc
    ]
    plane = [
        (ys[dy], xs[dx] * 16 + ys[dy] * 4 + low * 2 + core) for dx in far for dy in far if dx or dy
    ]
    beside = x * 16 + y * 4 + (1 - low) * 2 + core
    sibling = x * 16 + y * 4 + low * 2 + 1 - core

    barrier = pltpu.get_barrier_semaphore()
    for dz in range(8):
        for dy in range(4):
            to_state, to_low = lax.div(zs[dz], 2), lax.rem(zs[dz], 2)
            if dz >= 2 and dz <= 6:
                to_seq = x * 16 + ys[dy] * 4 + to_low * 2 + core
                pl.semaphore_signal(barrier, 1, device_id=(to_seq, to_state), device_id_type=MESH)
    to_z = lax.rem(state * 2 + low + jnp.where(low == 0, 7, 1), 8)
    for dy in range(4):
        to_seq = x * 16 + ys[dy] * 4 + lax.rem(to_z, 2) * 2 + core
        pl.semaphore_signal(barrier, 1, device_id=(to_seq, lax.div(to_z, 2)), device_id_type=MESH)
    for to_seq in mates:
        pl.semaphore_signal(barrier, 1, device_id=(to_seq, state), device_id_type=MESH)
    greeted = 5 * 4 + 4 + len(mates)

    def copy(src, dst, send_to, recv_on, to_seq, to_state=state):
        pltpu.make_async_remote_copy(
            src_ref=src, dst_ref=dst, send_sem=send_to, recv_sem=recv_on,
            device_id=(to_seq, to_state), device_id_type=MESH,
        ).start()

    def wait_bytes(ref, sem):
        pltpu.make_async_copy(ref, ref, sem).wait()

    def send(slot):
        for to, to_seq, to_state in peers:
            copy(sent.at[slot, to], received.at[slot, me], send_sem.at[slot], recv_sem.at[slot], to_seq, to_state)
        received[slot, pl.ds(me, 1)] = sent[slot, pl.ds(me, 1)]

    def wait(slot):
        wait_bytes(received.at[slot, pl.ds(0, PEERS - 1)], recv_sem.at[slot])

    def whole(ref, rows=slice(None)):
        return jnp.concatenate([ref[0, rows, :], ref[1, rows, :]], axis=1)

    def put(ref, a, rows=slice(None)):
        ref[0, rows, :] = a[:, :128]
        ref[1, rows, :] = a[:, 128:]

    low_half = iota((128, 128), 1) < 64

    def swap(a):
        return pltpu.roll(a, 64, 1)

    def at_inner(slot):
        a = [received[slot, s * GROUP : (s + 1) * GROUP].astype(F32).reshape(128, 128) for s in range(4)]
        top = [jnp.where(low_half, a[0], swap(a[1])), jnp.where(low_half, a[2], swap(a[3]))]
        bottom = [jnp.where(low_half, swap(a[0]), a[1]), jnp.where(low_half, swap(a[2]), a[3])]
        return jnp.concatenate([jnp.concatenate(top, axis=1), jnp.concatenate(bottom, axis=1)], axis=0)

    def from_inner(o, slot):
        for u in range(2):
            even, odd = o[:128, u * 128 : (u + 1) * 128], o[128:, u * 128 : (u + 1) * 128]
            first = jnp.where(low_half, even, swap(odd))
            second = jnp.where(low_half, swap(even), odd)
            sent[slot, 2 * u * GROUP : (2 * u + 1) * GROUP] = first.astype(BF16).reshape(GROUP, 16, 128)
            sent[slot, (2 * u + 1) * GROUP : (2 * u + 2) * GROUP] = second.astype(BF16).reshape(GROUP, 16, 128)

    def through_inner(a, factor):
        block = lax.rem(iota((256, 256), 0), 8)
        spread = jnp.concatenate([jnp.where(block == b, a, 0.0).astype(BF16) for b in range(8)], axis=1)
        return jnp.dot(spread, factor[...], preferred_element_type=F32)

    def at_outer(slot):
        a = received[slot].astype(F32)
        both = jnp.concatenate([a[:, :8].reshape(256, 128), a[:, 8:].reshape(256, 128)], axis=1)
        return both.T

    def from_outer(a, slot):
        t = a.T.reshape(PEERS, 8, 256)
        sent[slot] = jnp.concatenate([t[:, :, :128], t[:, :, 128:]], axis=1).astype(BF16)

    def through_outer(factor):
        def sixteen(g, carry):
            parts = [whole(rows_in, pl.ds(pl.multiple_of(n * 64 + g * 16, 16), 16)) for n in range(4)]
            part = jnp.concatenate(parts, axis=0)
            block = lax.rem(iota((64, 256), 0), 16)
            spread = jnp.concatenate([jnp.where(block == b, part, 0.0).astype(BF16) for b in range(16)], axis=1)
            o = jnp.dot(
                spread, factor[pl.ds(pl.multiple_of(g * 4096, 4096), 4096), :], preferred_element_type=F32
            )
            for n in range(4):
                put(rows_out, o[n * 16 : (n + 1) * 16], pl.ds(pl.multiple_of(n * 64 + g * 16, 16), 16))
            return carry

        lax.fori_loop(0, 4, sixteen, 0)

    def reweight(a, step):
        scaled = a * whole(emis.at[step])
        return jnp.concatenate(
            [scaled[n * 64 : (n + 1) * 64] / jnp.full((64, 256), norm_ref[step, n], F32) for n in range(4)], axis=0
        )

    def unfold(part, dst):
        def one(k, carry):
            for half in range(2):
                at = pl.ds(pl.multiple_of(k * 256 + half * 128, 128), 128)
                dst[half, pl.ds(k, 4, stride=64), :] = part(at).astype(F32)
            return carry

        lax.fori_loop(0, 64, one, 0, unroll=4)

    def spread_rows(a, slot):
        put(mixed, a)
        for b in range(GROUP):
            rows_sent[slot, b] = whole(mixed, pl.ds(b, 32, stride=8)).astype(BF16)
        for to, to_seq in sharers:
            copy(rows_sent.at[slot, to], rows_received.at[slot, share], rows_send.at[slot], rows_recv.at[slot], to_seq)
        rows_received[slot, pl.ds(share, 1)] = rows_sent[slot, pl.ds(share, 1)]

    for j in range(64):
        put(mixed, inner_ref[j].astype(F32), slice(j * 4, (j + 1) * 4))
    slab[...] = whole(mixed).astype(BF16).reshape(GROUP, 32, 256)
    unfold(lambda at: beta_ref[:, at], rows_out)
    unfold(lambda at: emis_ref[STEPS - 1, :, at], emis.at[STEPS - 1])
    from_outer(reweight(whole(rows_out), STEPS - 1), 0)
    pl.semaphore_wait(barrier, greeted)

    for to_y in range(4):
        copy(slab.at[to_y * 2 + 1 - low], relay.at[to_y], relay_send, relay_recv, beside)
    send(0)
    own, other = low * 2 + core, (1 - low) * 2 + core
    for to_y, to_seq in plane:
        copy(slab.at[to_y * 2 + low], gathered.at[own, x * 4 + y], gather_send.at[0], gather_recv.at[0], to_seq)
    gathered[own, pl.ds(x * 4 + y, 1)] = slab[pl.ds(place, 1)]

    unfold(lambda at: alpha_ref[:, at], rows_in)
    load.wait()
    through_outer(outer_nat)
    from_outer(whole(rows_out), 8)
    send(8)

    wait_bytes(relay, relay_recv)
    for to_y, to_seq in plane:
        copy(relay.at[to_y], gathered.at[other, x * 4 + y], gather_send.at[1], gather_recv.at[1], to_seq)
    gathered[other, pl.ds(x * 4 + y, 1)] = relay[pl.ds(y, 1)]

    def turn(k, carry):
        at = pl.ds(pl.multiple_of(k * 256, 256), 256)
        outer_tr[at, :] = outer_nat[at, :].T
        return carry

    lax.fori_loop(0, 24, turn, 0)
    wait_bytes(gathered.at[own, pl.ds(0, 15)], gather_recv.at[0])
    copy(gathered.at[own], gathered.at[own], core_send.at[0], core_recv.at[0], sibling)
    lax.fori_loop(24, 64, turn, 0)
    wait_bytes(gathered.at[other, pl.ds(0, 15)], gather_recv.at[1])
    copy(gathered.at[other], gathered.at[other], core_send.at[1], core_recv.at[1], sibling)
    for t in range(STEPS - 1):
        unfold(lambda at, t=t: emis_ref[t, :, at], emis.at[t])
    wait_bytes(gathered.at[own], core_recv.at[0])
    wait_bytes(gathered.at[other], core_recv.at[1])

    r, c = iota((512, 512), 0), iota((512, 512), 1)
    move = jnp.where(c == r // 4 % 4 * 128 + r // 16 % 4 * 32 + r // 64 * 4 + r % 4, 1.0, 0.0).astype(BF16)
    for q in range(4):
        part = jnp.concatenate([gathered[lc, q * 4 : (q + 1) * 4].reshape(128, 256) for lc in range(4)], axis=0)
        o = jnp.dot(move, part, preferred_element_type=F32)
        for b in range(8):
            inner_nat[b * 256 + q * 64 : b * 256 + (q + 1) * 64, :] = o[b * 64 : (b + 1) * 64].astype(BF16)
    for b in range(8):
        inner_tr[b * 256 : (b + 1) * 256, :] = inner_nat[b * 256 : (b + 1) * 256, :].T

    def step(t, carry):
        wait(t)
        a = at_inner(t)
        from_inner(through_inner(a, inner_tr), 4 + t)
        send(4 + t)
        spread_rows(a, STEPS + STEPS - 1 - t)
        wait(8 + t)
        a = at_inner(8 + t)
        from_inner(through_inner(a, inner_nat), 12 + t)
        send(12 + t)
        spread_rows(a, t)
        wait(4 + t)
        put(rows_in, at_outer(4 + t))
        through_outer(outer_tr)
        from_outer(reweight(whole(rows_out), STEPS - 2 - t), t + 1)
        send(t + 1)
        wait(12 + t)
        put(rows_in, reweight(at_outer(12 + t), t))
        through_outer(outer_nat)
        from_outer(whole(rows_out), 9 + t)
        send(9 + t)
        return carry

    lax.fori_loop(0, STEPS - 1, step, 0)

    def term(t):
        for slot in (t, STEPS + t):
            wait_bytes(rows_received.at[slot, pl.ds(0, GROUP - 1)], rows_recv.at[slot])
        ins, outs = rows_received[t].reshape(256, 256), rows_received[STEPS + t].reshape(256, 256)
        return jnp.dot(ins.T, outs, preferred_element_type=F32)

    mixed_grad = term(1) + term(2)
    grad_sent[...] = mixed_grad.reshape(SEQ, 4, 256)

    last = STEPS - 1
    wait(last)
    a = at_inner(last)
    spread_rows(a, STEPS)
    from_inner(through_inner(a, inner_tr), 4 + last)
    send(4 + last)
    wait(8 + last)
    spread_rows(at_inner(8 + last), last)

    grad = (term(0) + term(last)).reshape(SEQ, 4, 256)
    grad_sent[...] = (grad_sent[...] + grad) * (1.0 / 32.0)
    to_row = place * GROUP + share
    for to_seq in mates:
        copy(grad_sent.at[to_seq], grad_out.at[to_row], grad_send, grad_recv, to_seq)
    keep = pltpu.make_async_copy(grad_sent.at[seq], grad_out.at[to_row], grad_own)
    keep.start()

    wait(4 + last)
    put(rows_in, at_outer(4 + last))
    through_outer(outer_tr)

    def fold(k, carry):
        for half in range(2):
            at = pl.ds(pl.multiple_of(k * 256 + half * 128, 128), 128)
            beta_out[:, at] = rows_out[half, pl.ds(k, 4, stride=64), :]
        return carry

    lax.fori_loop(0, 64, fold, 0, unroll=4)

    keep.wait()
    wait_bytes(grad_out.at[pl.ds(0, SEQ - 1)], grad_recv)
    for slot in range(15):
        wait_bytes(sent.at[slot, pl.ds(0, PEERS - 1)], send_sem.at[slot])
    for slot in range(2 * STEPS):
        wait_bytes(rows_sent.at[slot, pl.ds(0, GROUP - 1)], rows_send.at[slot])
    wait_bytes(relay, relay_send)
    for n in range(2):
        wait_bytes(gathered.at[n, pl.ds(0, 15)], gather_send.at[n])
        wait_bytes(gathered.at[n], core_send.at[n])
    wait_bytes(grad_sent.at[pl.ds(0, SEQ - 1)], grad_send)


def local(outer_factor, inner_factor, alpha_start, beta_end, emissions, normalizers):
    vmem, hbm = pl.BlockSpec(memory_space=pltpu.VMEM), pl.BlockSpec(memory_space=pl.ANY)
    dma = pltpu.SemaphoreType.DMA
    return pl.pallas_call(
        kernel,
        out_shape=(jax.ShapeDtypeStruct((4, 64 * 256), F32), jax.ShapeDtypeStruct((64, 4, 256), F32)),
        in_specs=[pl.BlockSpec(memory_space=pltpu.SMEM), hbm, vmem, vmem, vmem, vmem],
        out_specs=(vmem, hbm),
        scratch_shapes=[
            pltpu.VMEM((64 * 256, 256), BF16),
            pltpu.VMEM((64 * 256, 256), BF16),
            pltpu.VMEM((8 * 256, 256), BF16),
            pltpu.VMEM((8 * 256, 256), BF16),
            pltpu.VMEM((GROUP, 32, 256), BF16),
            pltpu.VMEM((4, 32, 256), BF16),
            pltpu.VMEM((4, 16, 32, 256), BF16),
            pltpu.VMEM((15, PEERS, 16, 128), BF16),
            pltpu.VMEM((15, PEERS, 16, 128), BF16),
            pltpu.VMEM((2 * STEPS, GROUP, 32, 256), BF16),
            pltpu.VMEM((2 * STEPS, GROUP, 32, 256), BF16),
            pltpu.VMEM((SEQ, 4, 256), F32),
            pltpu.VMEM((STEPS, 2, 256, 128), F32),
            pltpu.VMEM((2, 256, 128), F32),
            pltpu.VMEM((2, 256, 128), F32),
            pltpu.VMEM((2, 256, 128), F32),
            dma,
            dma((15,)),
            dma((15,)),
            dma,
            dma,
            dma((2,)),
            dma((2,)),
            dma((2,)),
            dma((2,)),
            dma((2 * STEPS,)),
            dma((2 * STEPS,)),
            dma,
            dma,
            dma,
        ],
        compiler_params=pltpu.CompilerParams(
            collective_id=0, has_side_effects=True, vmem_limit_bytes=56 * 1024 * 1024
        ),
    )(
        normalizers,
        outer_factor.reshape(64 * 256, 256),
        inner_factor,
        alpha_start,
        beta_end,
        emissions,
    )


def solution(mesh):
    placed = (
        P("state", None, None),
        P("state", "seq", None),
        P("seq", "state"),
        P("seq", "state"),
        P(None, "seq", "state"),
        P(None, "seq"),
    )
    return jax.shard_map(
        local,
        mesh=mesh,
        in_specs=placed,
        out_specs=(P("seq", "state"), P("state", "seq", None)),
        check_vma=False,
    )
```

time: 112 us -> 96.2 us (0.86)
  Pallas kernels: 100 us -> 92.1 us
  local copies, waits for them, and re-layouts: 10.5 us -> 3.34 us
    reshape x6 -> x0, local copies, waits for them, and re-layouts: 10.5 us -> none  [the longest x1 2.18 us: local(): emissions.reshape(STEPS, 256, 256)]
    pallas_call x1, Pallas kernels: 100 us -> 92.1 us  [local(): pl.pallas_call(kernel, out_shape=(jax.ShapeDtypeStruct((4, 64 * 256), F32...]
    unnamed x0 -> x2, local copies, waits for them, and re-layouts: none -> 3.34 us
where the time goes in v2:
time: 96.2 us; the launch traced here: 96.1 us
  Pallas kernels  92.1 us (96%)
  local copies, waits for them, and re-layouts  3.34 us (3%)
    pallas_call x1, Pallas kernels, local(): pl.pallas_call(kernel, out_shape=(jax.ShapeDtypeStruct((4, 64 * 256), F32...  92.1 us
    unnamed x2, local copies, waits for them, and re-layouts  3.34 us

profile of v2, /device:TPU:1, one launch (start us, length us, event | category | flops | bytes accessed | tf_op | source)
XLA Modules:
  0.0 96.1 jit_solution(5371719142513612013)
XLA Ops:
  0.6 92.1 %shard_map.77 = (f32[4,16384]{1,0:T(4,128)}, f32[64,4,256]{2,1,0:T(4,128)}) custom-call(f32[4,4]{1,0:T(4,128)} %norm_ref.1, bf16[16384,256]{1,0:T(8,128)(2,1)} %bitcast.1, bf16[64,4,256]{2,1,0:T(4,128)(2,1)} %inner_ref.1, bf16[4,16384]{1,0:T(4,128)(2,1)} %alpha_ref.1, bf16[4,16384]{1,0:T(4,128)(2,1)} %beta_ref.1, bf16[4,4,16384]{2,1,0:T(4,128)(2,1)} %emis_ref.1), custom_call_target="tpu_custom_call" | custom-call | tf_op jit(solution)/shard_map/pallas_call | solution.py:315
  92.7 1.7 %copy.10 = f32[4,16384]{1,0:T(4,128)} copy(f32[4,16384]{1,0:T(4,128)} %get-tuple-element.4) | data formatting | bytes 524288
  94.4 1.7 %copy.11 = f32[64,4,256]{2,1,0:T(4,128)} copy(f32[64,4,256]{2,1,0:T(4,128)} %get-tuple-element.5) | data formatting | bytes 524288

commit v3 on v2

v3 whole, which is shorter than its diff:
```python
import functools

import jax
import jax.numpy as jnp
from jax import lax
from jax.experimental import pallas as pl
from jax.experimental.pallas import tpu as pltpu
from jax.sharding import PartitionSpec as P

MESH = pl.DeviceIdType.MESH
F32, BF16 = jnp.float32, jnp.bfloat16

GROUP = 8
PEERS = 32
SEQ = 64
STEPS = 4


def iota(shape, dim):
    return lax.broadcasted_iota(jnp.int32, shape, dim)


def kernel(
    norm_hbm, outer_hbm, inner_hbm, alpha_hbm, beta_hbm, emis_hbm,
    beta_out, grad_out,
    norm_ref, inner_ref, alpha_ref, beta_ref, emis_ref,
    outer_nat, outer_tr, inner_nat, inner_tr, slab, gathered, sent, received, rows_sent, rows_received,
    grad_sent, emis, rows_in, rows_out, mixed,
    load_sem, send_sem, recv_sem, gather_send, gather_recv, core_send, core_recv,
    rows_send, rows_recv, grad_send, grad_recv, grad_own,
):
    seq, state = lax.axis_index("seq"), lax.axis_index("state")
    x = lax.div(seq, 16)
    y = lax.rem(lax.div(seq, 4), 4)
    low = lax.rem(lax.div(seq, 2), 2)
    core = lax.rem(seq, 2)
    place = y * 2 + low
    share = x * 2 + core
    me = state * GROUP + place

    xs = [lax.rem(x + d, 4) for d in range(4)]
    ys = [lax.rem(y + d, 4) for d in range(4)]
    lows = [low, 1 - low]
    cores = [core, 1 - core]
    opposite = lax.rem(state + 2, 4)
    pairs = [lax.div(opposite, 2), lax.div(state, 2)]

    def mate_of(s):
        return s + 1 - 2 * lax.rem(s, 2)

    orders = [
        [(opposite, 0), (opposite, 1), (mate_of(opposite), 0), (mate_of(opposite), 1)],
        [(mate_of(state), 0), (mate_of(state), 1), (state, 1), (state, 0)],
    ]
    far = (2, 1, 3, 0)
    peers = [
        [
            (to_state * GROUP + ys[dy] * 2 + lows[dl], x * 16 + ys[dy] * 4 + lows[dl] * 2 + core, to_state)
            for to_state, dl in order for dy in far if to_state is not state or dl or dy
        ]
        for order in orders
    ]
    mates = [
        xs[dx] * 16 + ys[dy] * 4 + lows[dl] * 2 + cores[dc]
        for dx in far for dy in far for dl in (1, 0) for dc in (1, 0) if dx or dy or dl or dc
    ]
    sharers = [
        (xs[dx] * 2 + cores[dc], xs[dx] * 16 + y * 4 + low * 2 + cores[dc])
        for dx in far for dc in (1, 0) if dx or dc
    ]
    alike = [
        (dl, ys[dy] * 2 + lows[dl], xs[dx] * 16 + ys[dy] * 4 + lows[dl] * 2 + core)
        for dl in (1, 0) for dx in far for dy in far if dl or dx or dy
    ]
    sibling = x * 16 + y * 4 + low * 2 + 1 - core

    barrier = pltpu.get_barrier_semaphore()
    greeted = 0
    for to_seq, to_state in [p[1:] for p in peers[0] + peers[1] if p[2] is not state] + [(m, state) for m in mates]:
        pl.semaphore_signal(barrier, 1, device_id=(to_seq, to_state), device_id_type=MESH)
        greeted += 1

    pieces = ((inner_hbm, inner_ref), (beta_hbm, beta_ref), (emis_hbm, emis_ref), (norm_hbm, norm_ref),
              (alpha_hbm, alpha_ref), (outer_hbm, outer_nat))
    loads = [pltpu.make_async_copy(src, dst, load_sem.at[i]) for i, (src, dst) in enumerate(pieces)]
    for load in loads:
        load.start()

    def copy(src, dst, send_to, recv_on, to_seq, to_state=state):
        pltpu.make_async_remote_copy(
            src_ref=src, dst_ref=dst, send_sem=send_to, recv_sem=recv_on,
            device_id=(to_seq, to_state), device_id_type=MESH,
        ).start()

    def wait_bytes(ref, sem):
        pltpu.make_async_copy(ref, ref, sem).wait()

    def send(slot, turn):
        for to, to_seq, to_state in peers[turn]:
            copy(sent.at[slot, to], received.at[slot, me], send_sem.at[slot], recv_sem.at[slot], to_seq, to_state)
        if turn == 1:
            received[slot, pl.ds(me, 1)] = sent[slot, pl.ds(me, 1)]

    def wait(slot):
        wait_bytes(received.at[slot, pl.ds(0, PEERS - 1)], recv_sem.at[slot])

    def whole(ref, rows=slice(None)):
        return jnp.concatenate([ref[0, rows, :], ref[1, rows, :]], axis=1)

    def put(ref, a, rows=slice(None)):
        ref[0, rows, :] = a[:, :128]
        ref[1, rows, :] = a[:, 128:]

    low_half = iota((128, 128), 1) < 64

    def swap(a):
        return pltpu.roll(a, 64, 1)

    def at_inner(slot):
        a = [received[slot, s * GROUP : (s + 1) * GROUP].astype(F32).reshape(128, 128) for s in range(4)]
        top = [jnp.where(low_half, a[0], swap(a[1])), jnp.where(low_half, a[2], swap(a[3]))]
        bottom = [jnp.where(low_half, swap(a[0]), a[1]), jnp.where(low_half, swap(a[2]), a[3])]
        return jnp.concatenate([jnp.concatenate(top, axis=1), jnp.concatenate(bottom, axis=1)], axis=0)

    def through_inner(a, factor, slot):
        block = lax.rem(iota((256, 256), 0), 8)
        spread = jnp.concatenate([jnp.where(block == b, a, 0.0).astype(BF16) for b in range(8)], axis=1)
        o = jnp.dot(spread, factor[...], preferred_element_type=F32)
        for u in range(2):
            even, odd = o[:128, u * 128 : (u + 1) * 128], o[128:, u * 128 : (u + 1) * 128]
            first = jnp.where(low_half, even, swap(odd))
            second = jnp.where(low_half, swap(even), odd)
            both = jnp.concatenate([first, second], axis=0).astype(BF16).reshape(2 * GROUP, 16, 128)
            sent[slot, 2 * u * GROUP : (2 * u + 2) * GROUP] = both
        for turn in range(2):
            send(slot, turn)

    def at_outer(slot):
        a = received[slot].astype(F32)
        both = jnp.concatenate([a[:, :8].reshape(256, 128), a[:, 8:].reshape(256, 128)], axis=1)
        return both.T

    def from_outer(a, slot, turn):
        t = a.T.reshape(2 * GROUP, 8, 256)
        both = jnp.concatenate([t[:, :, :128], t[:, :, 128:]], axis=1).astype(BF16)
        sent[slot, pl.ds(pl.multiple_of(pairs[turn] * 2 * GROUP, 2 * GROUP), 2 * GROUP)] = both
        send(slot, turn)

    def through_outer(factor, u):
        half = pl.ds(pl.multiple_of(u * 128, 128), 128)
        block = lax.rem(iota((64, 256), 0), 16)
        for g in range(4):
            part = jnp.concatenate([whole(rows_in, slice(n * 64 + g * 16, n * 64 + g * 16 + 16)) for n in range(4)], axis=0)
            spread = jnp.concatenate([jnp.where(block == b, part, 0.0).astype(BF16) for b in range(16)], axis=1)
            o = jnp.dot(spread, factor[g * 4096 : (g + 1) * 4096, half], preferred_element_type=F32)
            for n in range(4):
                rows_out[u, n * 64 + g * 16 : n * 64 + g * 16 + 16, :] = o[n * 16 : (n + 1) * 16]

    def outer_stage(factor, slot, step=None):
        for turn in range(2):
            u = pairs[turn]
            through_outer(factor, u)
            a = rows_out[u]
            from_outer(a if step is None else a * emis[step, u], slot, turn)

    def unfold(part, dst, scale=None):
        def one(k, carry):
            for half in range(2):
                a = part(pl.ds(pl.multiple_of(k * 256 + half * 128, 128), 128)).astype(F32)
                dst[half, pl.ds(k, 4, stride=64), :] = a if scale is None else a * scale
            return carry

        lax.fori_loop(0, 64, one, 0, unroll=4)

    def unfold_emissions(t):
        row = iota((4, 128), 0)
        norm = jnp.full((4, 128), norm_ref[t, 0], F32)
        for n in range(1, 4):
            norm = jnp.where(row == n, norm_ref[t, n], norm)
        unfold(lambda at: emis_ref[t, :, at], emis.at[t], 1.0 / norm)

    def spread_rows(a, slot):
        put(mixed, a)
        for b in range(GROUP):
            rows_sent[slot, b] = whole(mixed, pl.ds(b, 32, stride=8)).astype(BF16)
        for to, to_seq in sharers:
            copy(rows_sent.at[slot, to], rows_received.at[slot, share], rows_send.at[slot], rows_recv.at[slot], to_seq)
        rows_received[slot, pl.ds(share, 1)] = rows_sent[slot, pl.ds(share, 1)]

    last = STEPS - 1
    loads[0].wait()
    for j in range(64):
        put(mixed, inner_ref[j].astype(F32), slice(j * 4, (j + 1) * 4))
    slab[...] = whole(mixed).astype(BF16).reshape(GROUP, 32, 256)
    pl.semaphore_wait(barrier, greeted)

    own, other = low * 2 + core, (1 - low) * 2 + core
    for dl, to, to_seq in alike:
        copy(slab.at[to], gathered.at[own, x * 4 + y], gather_send.at[dl], gather_recv.at[dl], to_seq)
    gathered[own, pl.ds(x * 4 + y, 1)] = slab[pl.ds(place, 1)]

    for load in loads[1:4]:
        load.wait()
    unfold(lambda at: beta_ref[:, at], rows_out)
    unfold_emissions(last)
    for turn in range(2):
        u = pairs[turn]
        from_outer(rows_out[u] * emis[last, u], 0, turn)

    loads[4].wait()
    unfold(lambda at: alpha_ref[:, at], rows_in)
    loads[5].wait()
    outer_stage(outer_nat, 8)

    def turn_block(k, carry):
        at = pl.ds(pl.multiple_of(k * 256, 256), 256)
        outer_tr[at, :] = outer_nat[at, :].T
        return carry

    wait_bytes(gathered.at[own, pl.ds(0, 15)], gather_recv.at[0])
    copy(gathered.at[own], gathered.at[own], core_send.at[0], core_recv.at[0], sibling)
    lax.fori_loop(0, 16, turn_block, 0)
    wait_bytes(gathered.at[other], gather_recv.at[1])
    copy(gathered.at[other], gathered.at[other], core_send.at[1], core_recv.at[1], sibling)
    lax.fori_loop(16, 64, turn_block, 0)
    for t in range(last):
        unfold_emissions(t)
    wait_bytes(gathered.at[own], core_recv.at[0])
    wait_bytes(gathered.at[other], core_recv.at[1])

    r, c = iota((512, 512), 0), iota((512, 512), 1)
    move = jnp.where(c == r // 4 % 4 * 128 + r // 16 % 4 * 32 + r // 64 * 4 + r % 4, 1.0, 0.0).astype(BF16)
    for q in range(4):
        part = jnp.concatenate([gathered[lc, q * 4 : (q + 1) * 4].reshape(128, 256) for lc in range(4)], axis=0)
        o = jnp.dot(move, part, preferred_element_type=F32)
        for b in range(8):
            inner_nat[b * 256 + q * 64 : b * 256 + (q + 1) * 64, :] = o[b * 64 : (b + 1) * 64].astype(BF16)
    for b in range(8):
        inner_tr[b * 256 : (b + 1) * 256, :] = inner_nat[b * 256 : (b + 1) * 256, :].T

    def step(t, carry):
        wait(t)
        a = at_inner(t)
        through_inner(a, inner_tr, 4 + t)
        spread_rows(a, STEPS + last - t)
        wait(8 + t)
        a = at_inner(8 + t)
        through_inner(a, inner_nat, 12 + t)
        spread_rows(a, t)
        wait(4 + t)
        put(rows_in, at_outer(4 + t))
        outer_stage(outer_tr, t + 1, last - 1 - t)
        wait(12 + t)
        put(rows_in, at_outer(12 + t) * whole(emis.at[t]))
        outer_stage(outer_nat, 9 + t)
        return carry

    lax.fori_loop(0, STEPS - 1, step, 0)

    def term(t):
        for slot in (t, STEPS + t):
            wait_bytes(rows_received.at[slot, pl.ds(0, GROUP - 1)], rows_recv.at[slot])
        ins, outs = rows_received[t].reshape(256, 256), rows_received[STEPS + t].reshape(256, 256)
        return jnp.dot(ins.T, outs, preferred_element_type=F32)

    mixed_grad = term(1) + term(2)
    grad_sent[...] = mixed_grad.reshape(SEQ, 4, 256)

    wait(last)
    a = at_inner(last)
    through_inner(a, inner_tr, 4 + last)
    spread_rows(a, STEPS)
    wait(8 + last)
    spread_rows(at_inner(8 + last), last)

    grad = (term(0) + term(last)).reshape(SEQ, 4, 256)
    grad_sent[...] = (grad_sent[...] + grad) * (1.0 / 32.0)
    to_row = place * GROUP + share
    for to_seq in mates:
        copy(grad_sent.at[to_seq], grad_out.at[to_row], grad_send, grad_recv, to_seq)
    keep = pltpu.make_async_copy(grad_sent.at[seq], grad_out.at[to_row], grad_own)
    keep.start()

    wait(4 + last)
    put(rows_in, at_outer(4 + last))
    for u in range(2):
        through_outer(outer_tr, u)

    def fold(k, carry):
        for half in range(2):
            at = pl.ds(pl.multiple_of(k * 256 + half * 128, 128), 128)
            beta_out[:, at] = rows_out[half, pl.ds(k, 4, stride=64), :]
        return carry

    lax.fori_loop(0, 64, fold, 0, unroll=4)

    keep.wait()
    wait_bytes(grad_out.at[pl.ds(0, SEQ - 1)], grad_recv)
    for slot in range(15):
        wait_bytes(sent.at[slot, pl.ds(0, PEERS - 1)], send_sem.at[slot])
    for slot in range(2 * STEPS):
        wait_bytes(rows_sent.at[slot, pl.ds(0, GROUP - 1)], rows_send.at[slot])
    wait_bytes(gathered.at[0, pl.ds(0, 15)], gather_send.at[0])
    wait_bytes(gathered.at[0], gather_send.at[1])
    for n in range(2):
        wait_bytes(gathered.at[n], core_send.at[n])
    wait_bytes(grad_sent.at[pl.ds(0, SEQ - 1)], grad_send)


def finish(beta, grad, beta_out, grad_out):
    beta_out[...] = beta[...]
    grad_out[...] = grad[...]


def local(outer_factor, inner_factor, alpha_start, beta_end, emissions, normalizers):
    vmem, hbm = pl.BlockSpec(memory_space=pltpu.VMEM), pl.BlockSpec(memory_space=pl.ANY)
    dma = pltpu.SemaphoreType.DMA
    results = (jax.ShapeDtypeStruct((4, 64 * 256), F32), jax.ShapeDtypeStruct((64, 4, 256), F32))
    beta_start, grad = pl.pallas_call(
        kernel,
        out_shape=results,
        in_specs=[hbm] * 6,
        out_specs=(vmem, hbm),
        scratch_shapes=[
            pltpu.SMEM((STEPS, 4), F32),
            pltpu.VMEM((64, 4, 256), BF16),
            pltpu.VMEM((4, 64 * 256), BF16),
            pltpu.VMEM((4, 64 * 256), BF16),
            pltpu.VMEM((STEPS, 4, 64 * 256), BF16),
            pltpu.VMEM((64 * 256, 256), BF16),
            pltpu.VMEM((64 * 256, 256), BF16),
            pltpu.VMEM((8 * 256, 256), BF16),
            pltpu.VMEM((8 * 256, 256), BF16),
            pltpu.VMEM((GROUP, 32, 256), BF16),
            pltpu.VMEM((4, 16, 32, 256), BF16),
            pltpu.VMEM((15, PEERS, 16, 128), BF16),
            pltpu.VMEM((15, PEERS, 16, 128), BF16),
            pltpu.VMEM((2 * STEPS, GROUP, 32, 256), BF16),
            pltpu.VMEM((2 * STEPS, GROUP, 32, 256), BF16),
            pltpu.VMEM((SEQ, 4, 256), F32),
            pltpu.VMEM((STEPS, 2, 256, 128), F32),
            pltpu.VMEM((2, 256, 128), F32),
            pltpu.VMEM((2, 256, 128), F32),
            pltpu.VMEM((2, 256, 128), F32),
            dma((6,)),
            dma((15,)),
            dma((15,)),
            dma((2,)),
            dma((2,)),
            dma((2,)),
            dma((2,)),
            dma((2 * STEPS,)),
            dma((2 * STEPS,)),
            dma,
            dma,
            dma,
        ],
        compiler_params=pltpu.CompilerParams(
            collective_id=0, has_side_effects=True, vmem_limit_bytes=56 * 1024 * 1024
        ),
    )(
        normalizers,
        outer_factor.reshape(64 * 256, 256),
        inner_factor,
        alpha_start,
        beta_end,
        emissions,
    )
    return pl.pallas_call(
        finish,
        out_shape=results,
        in_specs=[vmem, vmem],
        out_specs=(vmem, vmem),
    )(beta_start, grad)


def solution(mesh):
    placed = (
        P("state", None, None),
        P("state", "seq", None),
        P("seq", "state"),
        P("seq", "state"),
        P(None, "seq", "state"),
        P(None, "seq"),
    )
    return jax.shard_map(
        local,
        mesh=mesh,
        in_specs=placed,
        out_specs=(P("seq", "state"), P("state", "seq", None)),
        check_vma=False,
    )
```

time: 96.2 us -> 90.1 us (0.937)
  local copies, waits for them, and re-layouts: 3.34 us -> 0 us
  Pallas kernels: 92.1 us -> 89.3 us
    unnamed x2 -> x0, local copies, waits for them, and re-layouts: 3.34 us -> none
    pallas_call x1 -> x2, Pallas kernels: 92.1 us -> 89.3 us  [the longest x1 87.5 us: local(): pl.pallas_call(kernel, out_shape=results, in_specs=[hbm] * 6, out_specs=(...]
where the time goes in v3:
time: 90.1 us; the launch traced here: 90 us
  Pallas kernels  89.3 us (99%)
    pallas_call x1, Pallas kernels, local(): pl.pallas_call(kernel, out_shape=results, in_specs=[hbm] * 6, out_specs=(...  87.5 us
    pallas_call x1, Pallas kernels, local(): pl.pallas_call(finish, out_shape=results, in_specs=[vmem, vmem], out_spec...  1.84 us

profile of v3, /device:TPU:1, one launch (start us, length us, event | category | flops | bytes accessed | tf_op | source)
XLA Modules:
  0.0 90.0 jit_solution(13801742875799922413)
XLA Ops:
  0.6 87.5 %shard_map.77 = (f32[4,16384]{1,0:T(4,128)}, f32[64,4,256]{2,1,0:T(4,128)}) custom-call(f32[4,4]{1,0:T(4,128)} %norm_hbm.1, bf16[16384,256]{1,0:T(8,128)(2,1)} %bitcast.1, bf16[64,4,256]{2,1,0:T(4,128)(2,1)} %inner_hbm.1, bf16[4,16384]{1,0:T(4,128)(2,1)} %alpha_hbm.1, bf16[4,16384]{1,0:T(4,128)(2,1)} %beta_hbm.1, bf16[4,4,16384]{2,1,0:T(4,128)(2,1)} %emis_hbm.1), custom_call_target="tpu_custom_call" | custom-call | tf_op jit(solution)/shard_map/pallas_call | solution.py:319
  88.1 1.8 %shard_map.78 = (f32[4,16384]{1,0:T(4,128)}, f32[64,4,256]{2,1,0:T(4,128)}) custom-call(f32[4,16384]{1,0:T(4,128)} %get-tuple-element.4.beta, f32[64,4,256]{2,1,0:T(4,128)} %get-tuple-element.5.grad), custom_call_target="tpu_custom_call" | custom-call | tf_op jit(solution)/shard_map/pallas_call | solution.py:369

commit v4 on v3

--- a/solution.py
+++ b/solution.py
@@ -62,7 +62,7 @@
     ]
     mates = [
         xs[dx] * 16 + ys[dy] * 4 + lows[dl] * 2 + cores[dc]
-        for dx in far for dy in far for dl in (1, 0) for dc in (1, 0) if dx or dy or dl or dc
+        for dl in (1, 0) for dx in far for dy in far for dc in (1, 0) if dx or dy or dl or dc
     ]
     sharers = [
         (xs[dx] * 2 + cores[dc], xs[dx] * 16 + y * 4 + low * 2 + cores[dc])
@@ -140,11 +140,12 @@
         both = jnp.concatenate([a[:, :8].reshape(256, 128), a[:, 8:].reshape(256, 128)], axis=1)
         return both.T
 
-    def from_outer(a, slot, turn):
+    def from_outer(a, slot, turn, go=True):
         t = a.T.reshape(2 * GROUP, 8, 256)
         both = jnp.concatenate([t[:, :, :128], t[:, :, 128:]], axis=1).astype(BF16)
         sent[slot, pl.ds(pl.multiple_of(pairs[turn] * 2 * GROUP, 2 * GROUP), 2 * GROUP)] = both
-        send(slot, turn)
+        if go:
+            send(slot, turn)
 
     def through_outer(factor, u):
         half = pl.ds(pl.multiple_of(u * 128, 128), 128)
@@ -156,12 +157,12 @@
             for n in range(4):
                 rows_out[u, n * 64 + g * 16 : n * 64 + g * 16 + 16, :] = o[n * 16 : (n + 1) * 16]
 
-    def outer_stage(factor, slot, step=None):
+    def outer_stage(factor, slot, step=None, go=True):
         for turn in range(2):
             u = pairs[turn]
             through_outer(factor, u)
             a = rows_out[u]
-            from_outer(a if step is None else a * emis[step, u], slot, turn)
+            from_outer(a if step is None else a * emis[step, u], slot, turn, go)
 
     def unfold(part, dst, scale=None):
         def one(k, carry):
@@ -192,37 +193,44 @@
     for j in range(64):
         put(mixed, inner_ref[j].astype(F32), slice(j * 4, (j + 1) * 4))
     slab[...] = whole(mixed).astype(BF16).reshape(GROUP, 32, 256)
-    pl.semaphore_wait(barrier, greeted)
-
-    own, other = low * 2 + core, (1 - low) * 2 + core
-    for dl, to, to_seq in alike:
-        copy(slab.at[to], gathered.at[own, x * 4 + y], gather_send.at[dl], gather_recv.at[dl], to_seq)
-    gathered[own, pl.ds(x * 4 + y, 1)] = slab[pl.ds(place, 1)]
-
     for load in loads[1:4]:
         load.wait()
     unfold(lambda at: beta_ref[:, at], rows_out)
     unfold_emissions(last)
     for turn in range(2):
         u = pairs[turn]
-        from_outer(rows_out[u] * emis[last, u], 0, turn)
-
+        from_outer(rows_out[u] * emis[last, u], 0, turn, go=False)
     loads[4].wait()
     unfold(lambda at: alpha_ref[:, at], rows_in)
     loads[5].wait()
-    outer_stage(outer_nat, 8)
+    outer_stage(outer_nat, 8, go=False)
+    own, other = low * 2 + core, (1 - low) * 2 + core
+    gathered[own, pl.ds(x * 4 + y, 1)] = slab[pl.ds(place, 1)]
+    pl.semaphore_wait(barrier, greeted)
+
+    def send_slab(over):
+        for dl, to, to_seq in alike:
+            if dl == over:
+                copy(slab.at[to], gathered.at[own, x * 4 + y], gather_send.at[dl], gather_recv.at[dl], to_seq)
+
+    send_slab(1)
+    send(0, 0)
+    send(0, 1)
+    send_slab(0)
+    send(8, 0)
+    send(8, 1)
 
     def turn_block(k, carry):
         at = pl.ds(pl.multiple_of(k * 256, 256), 256)
         outer_tr[at, :] = outer_nat[at, :].T
         return carry
 
+    lax.fori_loop(0, 40, turn_block, 0)
     wait_bytes(gathered.at[own, pl.ds(0, 15)], gather_recv.at[0])
     copy(gathered.at[own], gathered.at[own], core_send.at[0], core_recv.at[0], sibling)
-    lax.fori_loop(0, 16, turn_block, 0)
+    lax.fori_loop(40, 64, turn_block, 0)
     wait_bytes(gathered.at[other], gather_recv.at[1])
     copy(gathered.at[other], gathered.at[other], core_send.at[1], core_recv.at[1], sibling)
-    lax.fori_loop(16, 64, turn_block, 0)
     for t in range(last):
         unfold_emissions(t)
     wait_bytes(gathered.at[own], core_recv.at[0])
@@ -281,21 +289,6 @@
     keep = pltpu.make_async_copy(grad_sent.at[seq], grad_out.at[to_row], grad_own)
     keep.start()
 
-    wait(4 + last)
-    put(rows_in, at_outer(4 + last))
-    for u in range(2):
-        through_outer(outer_tr, u)
-
-    def fold(k, carry):
-        for half in range(2):
-            at = pl.ds(pl.multiple_of(k * 256 + half * 128, 128), 128)
-            beta_out[:, at] = rows_out[half, pl.ds(k, 4, stride=64), :]
-        return carry
-
-    lax.fori_loop(0, 64, fold, 0, unroll=4)
-
-    keep.wait()
-    wait_bytes(grad_out.at[pl.ds(0, SEQ - 1)], grad_recv)
     for slot in range(15):
         wait_bytes(sent.at[slot, pl.ds(0, PEERS - 1)], send_sem.at[slot])
     for slot in range(2 * STEPS):
@@ -304,11 +297,29 @@
     wait_bytes(gathered.at[0], gather_send.at[1])
     for n in range(2):
         wait_bytes(gathered.at[n], core_send.at[n])
+
+    wait(4 + last)
+    put(rows_in, at_outer(4 + last))
+    stores = [pltpu.make_async_copy(rows_out.at[u], beta_out.at[u], load_sem.at[u]) for u in range(2)]
+    for u in range(2):
+        through_outer(outer_tr, u)
+        stores[u].start()
+
+    keep.wait()
     wait_bytes(grad_sent.at[pl.ds(0, SEQ - 1)], grad_send)
+    wait_bytes(grad_out.at[pl.ds(0, SEQ - 1)], grad_recv)
+    for store in stores:
+        store.wait()
 
 
 def finish(beta, grad, beta_out, grad_out):
-    beta_out[...] = beta[...]
+    def fold(k, carry):
+        for half in range(2):
+            at = pl.ds(pl.multiple_of(k * 256 + half * 128, 128), 128)
+            beta_out[:, at] = beta[half, pl.ds(k, 4, stride=64), :]
+        return carry
+
+    lax.fori_loop(0, 64, fold, 0, unroll=8)
     grad_out[...] = grad[...]
 
 
@@ -318,9 +329,9 @@
     results = (jax.ShapeDtypeStruct((4, 64 * 256), F32), jax.ShapeDtypeStruct((64, 4, 256), F32))
     beta_start, grad = pl.pallas_call(
         kernel,
-        out_shape=results,
+        out_shape=(jax.ShapeDtypeStruct((2, 256, 128), F32), results[1]),
         in_specs=[hbm] * 6,
-        out_specs=(vmem, hbm),
+        out_specs=(hbm, hbm),
         scratch_shapes=[
             pltpu.SMEM((STEPS, 4), F32),
             pltpu.VMEM((64, 4, 256), BF16),

time: 90.1 us -> 88.8 us (0.986)
  Pallas kernels: 89.3 us -> 88.1 us
    pallas_call x1, Pallas kernels: 87.5 us -> 86 us  [local(): pl.pallas_call(kernel, out_shape=(jax.ShapeDtypeStruct((2, 256, 128), F32...]
where the time goes in v4:
time: 88.8 us; the launch traced here: 88.7 us
  Pallas kernels  88.1 us (99%)
    pallas_call x1, Pallas kernels, local(): pl.pallas_call(kernel, out_shape=(jax.ShapeDtypeStruct((2, 256, 128), F32...  86 us
    pallas_call x1, Pallas kernels, local(): pl.pallas_call(finish, out_shape=results, in_specs=[vmem, vmem], out_spec...  2.05 us

profile of v4, /device:TPU:1, one launch (start us, length us, event | category | flops | bytes accessed | tf_op | source)
XLA Modules:
  0.0 88.7 jit_solution(16643494403682288934)
XLA Ops:
  0.6 86.0 %shard_map.77 = (f32[2,256,128]{2,1,0:T(8,128)}, f32[64,4,256]{2,1,0:T(4,128)}) custom-call(f32[4,4]{1,0:T(4,128)} %norm_hbm.1, bf16[16384,256]{1,0:T(8,128)(2,1)} %bitcast.1, bf16[64,4,256]{2,1,0:T(4,128)(2,1)} %inner_hbm.1, bf16[4,16384]{1,0:T(4,128)(2,1)} %alpha_hbm.1, bf16[4,16384]{1,0:T(4,128)(2,1)} %beta_hbm.1, bf16[4,4,16384]{2,1,0:T(4,128)(2,1)} %emis_hbm.1), custom_call_target="tpu_custom_call" | custom-call | tf_op jit(solution)/shard_map/pallas_call | solution.py:330
  86.7 2.1 %shard_map.78 = (f32[4,16384]{1,0:T(4,128)}, f32[64,4,256]{2,1,0:T(4,128)}) custom-call(f32[2,256,128]{2,1,0:T(8,128)} %get-tuple-element.4.beta, f32[64,4,256]{2,1,0:T(4,128)} %get-tuple-element.5.grad), custom_call_target="tpu_custom_call" | custom-call | tf_op jit(solution)/shard_map/pallas_call | solution.py:380

commit v5 on v4

--- a/solution.py
+++ b/solution.py
@@ -25,7 +25,7 @@
     beta_out, grad_out,
     norm_ref, inner_ref, alpha_ref, beta_ref, emis_ref,
     outer_nat, outer_tr, inner_nat, inner_tr, slab, gathered, sent, received, rows_sent, rows_received,
-    grad_sent, emis, rows_in, rows_out, mixed,
+    grad_early, grad_sent, emis, rows_in, rows_out, mixed,
     load_sem, send_sem, recv_sem, gather_send, gather_recv, core_send, core_recv,
     rows_send, rows_recv, grad_send, grad_recv, grad_own,
 ):
@@ -272,17 +272,17 @@
         return jnp.dot(ins.T, outs, preferred_element_type=F32)
 
     mixed_grad = term(1) + term(2)
-    grad_sent[...] = mixed_grad.reshape(SEQ, 4, 256)
+    grad_early[...] = mixed_grad.reshape(SEQ, 4, 256)
 
     wait(last)
     a = at_inner(last)
+    spread_rows(a, STEPS)
     through_inner(a, inner_tr, 4 + last)
-    spread_rows(a, STEPS)
     wait(8 + last)
     spread_rows(at_inner(8 + last), last)
 
     grad = (term(0) + term(last)).reshape(SEQ, 4, 256)
-    grad_sent[...] = (grad_sent[...] + grad) * (1.0 / 32.0)
+    grad_sent[...] = ((grad_early[...] + grad) * (1.0 / 32.0)).astype(BF16)
     to_row = place * GROUP + share
     for to_seq in mates:
         copy(grad_sent.at[to_seq], grad_out.at[to_row], grad_send, grad_recv, to_seq)
@@ -320,7 +320,7 @@
         return carry
 
     lax.fori_loop(0, 64, fold, 0, unroll=8)
-    grad_out[...] = grad[...]
+    grad_out[...] = grad[...].astype(F32)
 
 
 def local(outer_factor, inner_factor, alpha_start, beta_end, emissions, normalizers):
@@ -329,7 +329,7 @@
     results = (jax.ShapeDtypeStruct((4, 64 * 256), F32), jax.ShapeDtypeStruct((64, 4, 256), F32))
     beta_start, grad = pl.pallas_call(
         kernel,
-        out_shape=(jax.ShapeDtypeStruct((2, 256, 128), F32), results[1]),
+        out_shape=(jax.ShapeDtypeStruct((2, 256, 128), F32), jax.ShapeDtypeStruct((64, 4, 256), BF16)),
         in_specs=[hbm] * 6,
         out_specs=(hbm, hbm),
         scratch_shapes=[
@@ -349,6 +349,7 @@
             pltpu.VMEM((2 * STEPS, GROUP, 32, 256), BF16),
             pltpu.VMEM((2 * STEPS, GROUP, 32, 256), BF16),
             pltpu.VMEM((SEQ, 4, 256), F32),
+            pltpu.VMEM((SEQ, 4, 256), BF16),
             pltpu.VMEM((STEPS, 2, 256, 128), F32),
             pltpu.VMEM((2, 256, 128), F32),
             pltpu.VMEM((2, 256, 128), F32),

time: 88.8 us -> 88.2 us (level)
  no operation moved by 1% of the time
where the time goes in v5:
time: 88.2 us; the launch traced here: 88.1 us
  Pallas kernels  87.4 us (99%)
    pallas_call x1, Pallas kernels, local(): pl.pallas_call(kernel, out_shape=(jax.ShapeDtypeStruct((2, 256, 128), F32...  85.4 us
    pallas_call x1, Pallas kernels, local(): pl.pallas_call(finish, out_shape=results, in_specs=[vmem, vmem], out_spec...  2.01 us

profile of v5, /device:TPU:1, one launch (start us, length us, event | category | flops | bytes accessed | tf_op | source)
XLA Modules:
  0.0 88.1 jit_solution(8615996115271211785)
XLA Ops:
  0.6 85.4 %shard_map.77 = (f32[2,256,128]{2,1,0:T(8,128)}, bf16[64,4,256]{2,1,0:T(4,128)(2,1)}) custom-call(f32[4,4]{1,0:T(4,128)} %norm_hbm.1, bf16[16384,256]{1,0:T(8,128)(2,1)} %bitcast.1, bf16[64,4,256]{2,1,0:T(4,128)(2,1)} %inner_hbm.1, bf16[4,16384]{1,0:T(4,128)(2,1)} %alpha_hbm.1, bf16[4,16384]{1,0:T(4,128)(2,1)} %beta_hbm.1, bf16[4,4,16384]{2,1,0:T(4,128)(2,1)} %emis_hbm.1), custom_call_target="tpu_custom_call" | custom-call | tf_op jit(solution)/shard_map/pallas_call | solution.py:330
  86.1 2.0 %shard_map.78 = (f32[4,16384]{1,0:T(4,128)}, f32[64,4,256]{2,1,0:T(4,128)}) custom-call(f32[2,256,128]{2,1,0:T(8,128)} %get-tuple-element.4.beta, bf16[64,4,256]{2,1,0:T(4,128)(2,1)} %get-tuple-element.5.grad), custom_call_target="tpu_custom_call" | custom-call | tf_op jit(solution)/shard_map/pallas_call | solution.py:381
